TPU v7x, 128 devices: a whole 4x4x4 slice. The times are simulated.
128 devices in a mesh: node: 8 (over z, core), local: 16 (over x, y).
Axes of the slice: x: 4, y: 4, z: 4, core: 2. Of those that a mesh axis runs over, the one named last changes fastest.
Arguments:
- tokens: bfloat16 [256, 7168], P(('node', 'local')), may hold values from -6 to 6
- gates: bfloat16 [256, 8], P(('node', 'local')), may hold values from 0.049804688 to 0.5
- node_set: int32 [256, 4], P(('node', 'local')), may hold values from 0 to 7, all different within a row; in each aligned block of 2 rows (0 to 1, 2 to 3, ...) at most 2 rows name the same one
- w_gate: bfloat16 [7168, 32768], P(None, ('node', 'local')), may hold values from -0.0625 to 0.0625
- w_up: bfloat16 [7168, 32768], P(None, ('node', 'local')), may hold values from -0.0625 to 0.0625
- w_down: bfloat16 [32768, 7168], P(('node', 'local')), may hold values from -0.125 to 0.125
Outputs:
- mixed: bfloat16 [256, 7168], P(('node', 'local'))
Inputs may be any that keep to these rules, and one draw needn't show every extreme that they name: `node_set`: each row names 4 different nodes; among the rows of one device at most 2 name the same node, and in every draw some node is named by exactly 2 rows of some device.
All inputs are finite; a program needn't handle non-finite values.
Results may differ from a plain program's by a relative error of at most 0.005.
Values may be sent and summed in bfloat16 or wider, within the bound.
A program may use at most 64 MiB of HBM per device.

v0:
```python
import jax
import jax.numpy as jnp
from jax import lax
from jax.sharding import PartitionSpec as P

FF = 2048


def expert_output(rows_in, rows_gate, own_expert, part_gate, part_up, part_down):
    node_experts = rows_gate.shape[1]
    pick_column = (jnp.arange(node_experts, dtype=jnp.int32) == own_expert).astype(jnp.float32)
    gate_column = jnp.sum(rows_gate.astype(jnp.float32) * pick_column[None, :], axis=1)
    gate_pre = jnp.dot(rows_in, part_gate, preferred_element_type=jnp.float32)
    up_pre = jnp.dot(rows_in, part_up, preferred_element_type=jnp.float32)
    hidden_act = (gate_pre * jax.nn.sigmoid(gate_pre) * up_pre).astype(jnp.bfloat16)
    expert_out = jnp.dot(hidden_act, part_down, preferred_element_type=jnp.float32)
    return gate_column[:, None] * expert_out


def route_tables(node_set, gates, node_count, capacity, node_experts):
    tok_rows, node_limit = node_set.shape
    node_ids = jnp.arange(node_count, dtype=jnp.int32)
    node_match = node_set[:, :, None] == node_ids[None, None, :]
    node_hit = node_match.astype(jnp.float32)
    chosen = jnp.sum(node_match.astype(jnp.int32), axis=1)
    slot_rank = jnp.cumsum(chosen, axis=0) - chosen
    slot_ids = jnp.arange(capacity, dtype=jnp.int32)
    slot_match = (slot_rank[:, :, None] == slot_ids[None, None, :]) & (chosen[:, :, None] > 0)
    placement = slot_match.astype(jnp.float32)
    gate_table = gates.astype(jnp.float32).reshape(tok_rows, node_limit, node_experts)
    per_node = jnp.einsum("tjn,tje->tne", node_hit, gate_table)
    slot_gates = jnp.einsum("tnc,tne->nce", placement, per_node).astype(jnp.bfloat16)
    return (placement.reshape(tok_rows, node_count * capacity), slot_gates)


def body(tokens, gates, node_set, w_gate, w_up, w_down):
    node_count = lax.axis_size("node")
    local_count = lax.axis_size("local")
    tok_rows, model_width = tokens.shape
    hidden = w_gate.shape[1]
    slices = FF // hidden
    node_experts = local_count // slices
    node_limit = node_set.shape[1]
    capacity = min(tok_rows, (5 * tok_rows * node_limit + 4 * node_count - 1) // (4 * node_count))
    own_expert = lax.axis_index("local") // slices
    placement, slot_gates = route_tables(node_set, gates, node_count, capacity, node_experts)
    place_half = placement.astype(jnp.bfloat16)
    send_in = jnp.einsum(
        "ts,td->sd", place_half, tokens, preferred_element_type=jnp.float32
    ).astype(jnp.bfloat16)
    send_in = send_in.reshape(node_count, capacity, model_width)
    wide_shape = (node_count, local_count, capacity, model_width)
    flat_shape = (node_count * local_count, capacity, model_width)
    wide_in = jnp.broadcast_to(send_in[:, None], wide_shape).reshape(flat_shape)
    wide_gate = jnp.broadcast_to(
        slot_gates[:, None], (node_count, local_count, capacity, node_experts)
    )
    wide_gate = wide_gate.reshape(node_count * local_count, capacity, node_experts)
    rows_in, rows_gate = (
        lax.all_to_all(wide_in, ("node", "local"), split_axis=0, concat_axis=0, tiled=True),
        lax.all_to_all(wide_gate, ("node", "local"), split_axis=0, concat_axis=0, tiled=True),
    )
    partial_value = expert_output(
        rows_in.reshape(-1, model_width),
        rows_gate.reshape(-1, node_experts),
        own_expert,
        w_gate,
        w_up,
        w_down,
    )
    arrived = lax.all_to_all(
        partial_value.reshape(flat_shape),
        ("node", "local"),
        split_axis=0,
        concat_axis=0,
        tiled=True,
    )
    returned = jnp.sum(arrived.reshape(wide_shape), axis=1)
    mixed_sum = jnp.einsum(
        "ts,sd->td", placement, returned.reshape(-1, model_width), precision=lax.Precision.HIGHEST
    )
    return mixed_sum.astype(jnp.bfloat16)


def solution(mesh):
    in_specs = (
        P(("node", "local"), None),
        P(("node", "local"), None),
        P(("node", "local"), None),
        P(None, ("node", "local")),
        P(None, ("node", "local")),
        P(("node", "local"), None),
    )
    out_specs = P(("node", "local"), None)
    return jax.shard_map(body, mesh=mesh, in_specs=in_specs, out_specs=out_specs, check_vma=False)
```

profile of v0, /device:TPU:1, one launch (start us, length us, event | category | flops | bytes accessed | tf_op | source)
XLA Modules:
  0.0 207.0 jit_solution(328526876356324391)
XLA Ops:
  0.0 0.8 convert_reduce_fusion
  0.8 0.7 reshape.53
  1.6 0.9 fusion.9
  2.4 0.1 copy.33
  2.5 0.1 copy.32
  2.7 0.1 fusion.17
  2.8 0.7 broadcast_in_dim.6
  3.5 11.5 %all-to-all-start = ((bf16[128,2,2]{2,1,0:T(2,128)(2,1)}), bf16[128,2,2]{2,1,0:T(2,128)(2,1)S(1)}, u32[]{:S(2)}, u32[]{:S(2)}) async-start(bf16[128,2,2]{2,1,0:T(2,128)(2,1)} %bitcast), calls=%async_computation | async-start | bytes 131072 | tf_op jit(solution)/shard_map/all_to_all | solution.py:61
  15.0 0.1 and.22
  15.4 0.3 convolution_convert_fusion
  15.6 0.1 broadcast_in_dim.7
  15.7 8.8 %all-to-all-done = bf16[128,2,2]{2,1,0:T(2,128)(2,1)S(1)} async-done(((bf16[128,2,2]{2,1,0:T(2,128)(2,1)}), bf16[128,2,2]{2,1,0:T(2,128)(2,1)S(1)}, u32[]{:S(2)}, u32[]{:S(2)}) %all-to-all-start) | async-done | bytes 1056 | tf_op jit(solution)/shard_map/all_to_all | solution.py:61
  24.5 3.7 %broadcast_in_dim.8 = bf16[8,16,2,7168]{3,2,1,0:T(2,128)(2,1)} broadcast(bf16[8,2,7168]{2,1,0:T(2,128)(2,1)S(1)} %broadcast_in_dim.7), dimensions={0,2,3} | broadcast | bytes 3899392 | tf_op jit(solution)/shard_map/broadcast_in_dim | solution.py:54
  28.3 5.4 %all-to-all-start.1 = ((bf16[128,2,7168]{2,1,0:T(2,128)(2,1)}), bf16[128,2,7168]{2,1,0:T(2,128)(2,1)}, u32[]{:S(2)}, u32[]{:S(2)}) async-start(bf16[128,2,7168]{2,1,0:T(2,128)(2,1)} %bitcast.17), calls=%async_computation.1 | async-start | bytes 7340032 | tf_op jit(solution)/shard_map/all_to_all | solution.py:60
  33.9 0.1 copy.35
  34.0 0.1 mul.27
  34.2 46.4 %all-to-all-done.1 = bf16[128,2,7168]{2,1,0:T(2,128)(2,1)} async-done(((bf16[128,2,7168]{2,1,0:T(2,128)(2,1)}), bf16[128,2,7168]{2,1,0:T(2,128)(2,1)}, u32[]{:S(2)}, u32[]{:S(2)}) %all-to-all-start.1) | async-done | bytes 3670048 | tf_op jit(solution)/shard_map/all_to_all | solution.py:60
  80.6 8.4 %reshape.56 = bf16[256,7168]{1,0:T(8,128)(2,1)} reshape(bf16[128,2,7168]{2,1,0:T(2,128)(2,1)} %all-to-all-done.1) | data formatting | bytes 7340032 | tf_op jit(solution)/shard_map/reshape | solution.py:64
  89.0 4.3 %fusion.16 = f32[256,256]{1,0:T(8,128)S(1)} fusion(bf16[256,7168]{1,0:T(8,128)(2,1)} %reshape.56, bf16[7168,256]{1,0:T(8,128)(2,1)} %param.9), kind=kOutput, calls=%fused_computation.28 | convolution fusion | flops 939524096 | bytes 7602176 | tf_op jit(solution)/shard_map/dot_general | solution.py:13
  93.2 11.2 %convolution_multiply_fusion = f32[256,7168]{1,0:T(8,128)} fusion(bf16[256,7168]{1,0:T(8,128)(2,1)} %param.11, f32[256]{0:T(256)S(1)} %mul.27, bf16[256,7168]{1,0:T(8,128)(2,1)} %reshape.56, bf16[7168,256]{1,0:T(8,128)(2,1)} %param.10, f32[256,256]{1,0:T(8,128)S(1)} %fusion.16), kind=kOutput, calls=%fused_computation | convolution fusion | flops 1881276416 | bytes 18613248 | tf_op jit(solution)/shard_map/dot_general | solution.py:16
  104.4 9.3 %reshape.57 = f32[128,2,7168]{2,1,0:T(2,128)} reshape(f32[256,7168]{1,0:T(8,128)} %convolution_multiply_fusion) | data formatting | bytes 14680064 | tf_op jit(solution)/shard_map/reshape | solution.py:72
  113.7 90.7 %all_to_all.15 = f32[128,2,7168]{2,1,0:T(2,128)S(1)} all-to-all(f32[128,2,7168]{2,1,0:T(2,128)} %reshape.57), channel_id=1, replica_groups=mesh['node'=8,'local'=16] {'node','local'}, dimensions={0} | all-to-all | bytes 14680064 | tf_op jit(solution)/shard_map/all_to_all | solution.py:71
  204.4 1.6 bitcast_reduce_fusion
  206.0 1.0 fusion
  (14 shorter events, 0.6 us)
Async XLA Ops:
  0.0 15.4 %copy-start = (bf16[2,7168]{1,0:T(2,128)(2,1)S(1)}, bf16[2,7168]{1,0:T(2,128)(2,1)}, u32[]{:S(2)}) copy-start(bf16[2,7168]{1,0:T(2,128)(2,1)} %param.6) | copy-start | bytes 86020
  3.5 21.1 %all-to-all-start = ((bf16[128,2,2]{2,1,0:T(2,128)(2,1)}), bf16[128,2,2]{2,1,0:T(2,128)(2,1)S(1)}, u32[]{:S(2)}, u32[]{:S(2)}) async-start(bf16[128,2,2]{2,1,0:T(2,128)(2,1)} %bitcast), calls=%async_computation | async-start | bytes 131072 | tf_op jit(solution)/shard_map/all_to_all | solution.py:61
  28.3 52.3 %all-to-all-start.1 = ((bf16[128,2,7168]{2,1,0:T(2,128)(2,1)}), bf16[128,2,7168]{2,1,0:T(2,128)(2,1)}, u32[]{:S(2)}, u32[]{:S(2)}) async-start(bf16[128,2,7168]{2,1,0:T(2,128)(2,1)} %bitcast.17), calls=%async_computation.1 | async-start | bytes 7340032 | tf_op jit(solution)/shard_map/all_to_all | solution.py:60
where the time goes:
time: 208 us; the launch traced here: 207 us
  blocking collectives  90.7 us (44%)
  waiting for transfers between devices  55.2 us (27%)
  local copies, waits for them, and re-layouts  23.8 us (11%)
  matrix products  17.7 us (9%)
  starting transfers between devices  16.9 us (8%)
  other arithmetic  2.49 us (1%)
    all_to_all x1, blocking collectives, body(): lax.all_to_all(partial_value.reshape(flat_shape), ('node', 'local'), spli...  90.7 us
    all_to_all x1, waiting for transfers between devices, body(): lax.all_to_all(wide_in, ('node', 'local'), split_axis=0, concat_axis=0, t...  46.4 us
    all_to_all x1, starting transfers between devices, body(): lax.all_to_all(wide_gate, ('node', 'local'), split_axis=0, concat_axis=0,...  11.5 us
    dot_general x1, matrix products, expert_output(): jnp.dot(hidden_act, part_down, preferred_element_type=jnp.float32)  11.2 us
    reshape x1, local copies, waits for them, and re-layouts, body(): partial_value.reshape(flat_shape)  9.26 us
    all_to_all x1, waiting for transfers between devices, body(): lax.all_to_all(wide_gate, ('node', 'local'), split_axis=0, concat_axis=0,...  8.79 us
    reshape x1, local copies, waits for them, and re-layouts, body(): rows_in.reshape(-1, model_width)  8.39 us
    all_to_all x1, starting transfers between devices, body(): lax.all_to_all(wide_in, ('node', 'local'), split_axis=0, concat_axis=0, t...  5.44 us
  transfers between devices with their start and end apart: 2, of which 2 were waited for; matrix products, arithmetic and copies ran while one was open for 1% of the time, Pallas kernels for 0%

commit v1 on v0

v1 whole, which is shorter than its diff:
```python
import functools

import jax
import jax.numpy as jnp
from jax import lax
from jax.experimental import pallas as pl
from jax.experimental.pallas import tpu as pltpu
from jax.sharding import PartitionSpec as P

MESH = pl.DeviceIdType.MESH
SIDE = 4
ROWS = 256
TOK = 2
LINE_ROWS = 16
PLANE_ROWS = 64
LANES = 128
AHEAD = (2, 1, 3, 0)
ORDERS = ("xyz", "yzx", "zxy")
UNITS = ((0, 10), (1, 9), (2, 9))
F32, BF16 = jnp.float32, jnp.bfloat16


def widths():
    offsets, start = [], 0
    for _, blocks in UNITS:
        offsets.append(start)
        start += 2 * blocks * LANES
    return offsets, [blocks * LANES for _, blocks in UNITS]


def row_of(order, at, by_plane):
    low = at & 3
    place = dict(x=(at >> 2) & 3, y=(at >> 4) & 3, z=(at >> 6) & 3)
    first, second, third = (place[axis] for axis in ORDERS[order])
    slow, fast = (third, second) if by_plane else (second, third)
    return (((slow * SIDE + fast) * SIDE + first) << 2) + low


def kernel(tok, gates, node_set, wg, wu, wd, out, **r):
    offsets, width = widths()
    n = len(UNITS)

    node, local = lax.axis_index("node"), lax.axis_index("local")
    here = dict(x=local // SIDE, y=local % SIDE, z=node // 2)
    core = node % 2

    def device(axis, step, flip):
        at = dict(here)
        at[axis] = lax.rem(at[axis] + step, SIDE)
        other = lax.rem(core + flip, 2)
        return (at["z"] * 2 + other, at["x"] * SIDE + at["y"])

    loads = [
        pltpu.make_async_copy(wg, r["wg_v"], r["load_sem"].at[0]),
        pltpu.make_async_copy(wu, r["wu_v"], r["load_sem"].at[1]),
        pltpu.make_async_copy(wd, r["wd_v"], r["load_sem"].at[2]),
    ]
    small = [
        pltpu.make_async_copy(gates, r["gates_v"], r["small_sem"].at[0]),
        pltpu.make_async_copy(node_set, r["set_v"], r["small_sem"].at[1]),
    ]
    own = []
    for u in range(n):
        for h in range(2):
            own.append(
                pltpu.make_async_copy(
                    tok.at[:, pl.ds(offsets[u] + h * width[u], width[u])],
                    r["src"][u].at[h, :, pl.ds(0, width[u])],
                    r["tok_sem"].at[u, h],
                )
            )
    for copy in small + own:
        copy.start()

    barrier = pltpu.get_barrier_semaphore()
    partners = [(axis, step, flip) for axis in "xyz" for step in range(1, SIDE) for flip in range(2)]
    partners.append(("x", 0, 1))
    for partner in partners:
        pl.semaphore_signal(barrier, inc=1, device_id=device(*partner), device_id_type=MESH)
    for copy in loads:
        copy.start()

    for copy in small:
        copy.wait()
    lane = lax.broadcasted_iota(jnp.int32, (TOK, LANES), 1)
    table = jnp.zeros((TOK, LANES), F32)
    gate_v, set_v = r["gates_v"][...].astype(F32), r["set_v"][...]
    for j in range(set_v.shape[1]):
        pair = jnp.where(lane % 2 == 0, gate_v[:, 2 * j : 2 * j + 1], gate_v[:, 2 * j + 1 : 2 * j + 2])
        table = table + jnp.where(set_v[:, j : j + 1] == lane // 2, pair, 0.0)
    for h in range(2):
        r["src"][0][h, :, width[0] :] = table.astype(BF16)
    for copy in own:
        copy.wait()
    pl.semaphore_wait(barrier, len(partners))


    def send(src, dst, send_sem, recv_sem, to):
        copy = pltpu.make_async_remote_copy(
            src_ref=src, dst_ref=dst, send_sem=send_sem, recv_sem=recv_sem, device_id=to, device_id_type=MESH
        )
        copy.start()

    def axes(u):
        return ORDERS[UNITS[u][0]]

    def line_slot(u):
        return here[axes(u)[0]] * 2 + core

    for u in range(n):
        for step in (1, 3, 2, 0):
            for flip in range(2):
                if step or flip:
                    send(
                        r["src"][u].at[lax.rem(core + flip, 2)],
                        r["line"][u].at[line_slot(u)],
                        r["p1_send"].at[u],
                        r["p1_recv"].at[u],
                        device(axes(u)[0], step, flip),
                    )
        r["line"][u][pl.ds(line_slot(u), 1)] = r["src"][u][pl.ds(core, 1)]

    def wait_all(ref, sem):
        pltpu.make_async_copy(ref, ref, sem).wait()

    down_at = lax.broadcasted_iota(jnp.int32, (ROWS, ROWS), 0)
    across = lax.broadcasted_iota(jnp.int32, (ROWS, ROWS), 1)
    for o in (1, 2):
        r["perm"][o - 1] = (row_of(o, down_at, True) == across).astype(F32).astype(BF16)
    for o in range(3):
        r["back"][o] = (row_of(o, across, False) == down_at).astype(F32).astype(BF16)
    def plane_row(u):
        return here[axes(u)[2]] * PLANE_ROWS

    def line_block(u, back):
        second = lax.rem(here[axes(u)[1]] + SIDE - back, SIDE)
        return r["rows"][u].at[0, pl.ds(pl.multiple_of(plane_row(u) + second * LINE_ROWS, LINE_ROWS), LINE_ROWS)]

    def plane_block(u, half, back):
        third = lax.rem(here[axes(u)[2]] + SIDE - back, SIDE)
        return r["rows"][u].at[half, pl.ds(pl.multiple_of(third * PLANE_ROWS, PLANE_ROWS), PLANE_ROWS)]

    def gather3(u, back):
        for step in (2, 1, 3):
            view = line_block(u, back)
            send(view, view, r["p3_send"].at[u], r["p3_recv"].at[u, step - 1], device(axes(u)[2], step, 0))

    for u in range(n):
        wait_all(r["line"][u].at[pl.ds(0, 7)], r["p1_recv"].at[u])
        block = jnp.concatenate([r["line"][u][i].astype(F32) for i in range(8)], axis=0)
        view = line_block(u, 0)
        view[...] = block.astype(BF16)
        for step in (2, 1, 3):
            send(view, view, r["p2_send"].at[u], r["p2_recv"].at[u, step - 1], device(axes(u)[1], step, 0))
    for u in range(n):
        gather3(u, 0)
    for step in (1, 3, 2):
        for u in range(n):
            wait_all(line_block(u, step), r["p2_recv"].at[u, step - 1])
            gather3(u, step)
    for step in (0, 1, 3, 2):
        for u in range(n):
            if step:
                wait_all(plane_block(u, 0, step), r["p3_recv"].at[u, step - 1])
            send(
                plane_block(u, 0, step),
                plane_block(u, 1, step),
                r["s_send"].at[u],
                r["s_recv"].at[u, step],
                device("x", 0, 1),
            )
    for copy in loads[:2]:
        copy.wait()
    for which in range(2):
        for u in range(n):
            if which:
                for step in range(SIDE):
                    wait_all(r["rows"][u].at[1, pl.ds(0, PLANE_ROWS)], r["s_recv"].at[u, step])
            half = core if which == 0 else 1 - core
            depth = pl.ds(pl.multiple_of(offsets[u] + half * width[u], LANES), width[u])
            lhs = r["rows"][u][which, :, : width[u]]
            o = UNITS[u][0]
            for side, weight in enumerate((r["wg_v"], r["wu_v"])):
                part = jnp.dot(lhs, weight[depth, :], preferred_element_type=F32)
                columns = slice(side * 256, side * 256 + 256)
                first = which == 0 and all(UNITS[v][0] != o for v in range(u))
                r["acc"][o, :, columns] = part if first else r["acc"][o, :, columns] + part

    expert = node * 2 + local // 8
    lane = lax.broadcasted_iota(jnp.int32, (ROWS, LANES), 1)
    table = r["rows"][0][0, :, width[0] :]
    for o in range(3):
        here_table = jnp.dot(r["back"][o], table, preferred_element_type=F32)
        column = jnp.sum(jnp.where(lane == expert, here_table, 0.0), axis=1, keepdims=True)
        r["gcol"][o] = jnp.broadcast_to(column, (ROWS, LANES))

    total = r["acc"][0]
    for o in (1, 2):
        high = r["acc"][o].astype(BF16)
        low = (r["acc"][o] - high.astype(F32)).astype(BF16)
        total = total + jnp.dot(r["perm"][o - 1], high, preferred_element_type=F32)
        total = total + jnp.dot(r["perm"][o - 1], low, preferred_element_type=F32)
    gate_pre, up_pre = total[:, :256], total[:, 256:]
    hidden = (gate_pre * jax.nn.sigmoid(gate_pre) * up_pre).astype(BF16)
    for o in range(3):
        r["hid"][o] = jnp.dot(r["back"][o], hidden, preferred_element_type=F32).astype(BF16)
    loads[2].wait()

    def down(u, half):
        o = UNITS[u][0]
        columns = pl.ds(pl.multiple_of(offsets[u] + half * width[u], LANES), width[u])
        part = jnp.dot(r["hid"][o], r["wd_v"][:, columns], preferred_element_type=F32)
        return part * r["gcol"][o][:, :1]

    def second_block(u, ahead):
        second = lax.rem(here[axes(u)[1]] + ahead, SIDE)
        return pl.ds(pl.multiple_of(second * PLANE_ROWS, PLANE_ROWS), PLANE_ROWS)

    def third_block(u, ahead, step):
        second = lax.rem(here[axes(u)[1]] + ahead, SIDE)
        third = lax.rem(here[axes(u)[2]] + step, SIDE)
        return pl.ds(pl.multiple_of(second * PLANE_ROWS + third * LINE_ROWS, LINE_ROWS), LINE_ROWS)

    for u in range(n):
        r["sib_out"][u][...] = down(u, 1 - core).astype(BF16)
    for ahead in AHEAD:
        for u in range(n):
            at = second_block(u, ahead)
            send(r["sib_out"][u].at[at], r["sib_in"][u].at[at], r["r0_send"].at[u], r["r0_recv"].at[u, ahead], device("x", 0, 1))
    for u in range(n):
        r["own"][u][...] = down(u, core)
    for ahead in AHEAD:
        for u in range(n):
            at = second_block(u, ahead)
            wait_all(r["sib_in"][u].at[at], r["r0_recv"].at[u, ahead])
            r["r1_src"][u][at, :] = (r["own"][u][at, :] + r["sib_in"][u][at, :].astype(F32)).astype(BF16)
            for step in (2, 1, 3):
                send(
                    r["r1_src"][u].at[third_block(u, ahead, step)],
                    r["r1_dst"][u].at[ahead, step - 1],
                    r["r1_send"].at[u],
                    r["r1_recv"].at[u, ahead],
                    device(axes(u)[2], step, 0),
                )
    for u in range(n):
        wait_all(r["line"][u].at[pl.ds(0, 7)], r["p1_send"].at[u])
        wait_all(r["rows"][u].at[0, pl.ds(0, 3 * LINE_ROWS)], r["p2_send"].at[u])
        wait_all(r["rows"][u].at[0, pl.ds(0, 3 * PLANE_ROWS)], r["p3_send"].at[u])
        wait_all(r["rows"][u].at[0], r["s_send"].at[u])
    for ahead in AHEAD:
        for u in range(n):
            at = third_block(u, ahead, 0)
            wait_all(r["r1_dst"][u].at[ahead], r["r1_recv"].at[u, ahead])
            part = r["own"][u][at, :] + r["sib_in"][u][at, :].astype(F32)
            for step in range(3):
                part = part + r["r1_dst"][u][ahead, step].astype(F32)
            if ahead:
                r["r2_src"][u][ahead - 1] = part.astype(BF16)
                send(
                    r["r2_src"][u].at[ahead - 1],
                    r["r2_dst"][u].at[ahead - 1],
                    r["r2_send"].at[u],
                    r["r2_recv"].at[u],
                    device(axes(u)[1], ahead, 0),
                )
            else:
                r["r2_own"][u][...] = part
    for u in range(n):
        wait_all(r["r2_dst"][u], r["r2_recv"].at[u])
        part = r["r2_own"][u][...]
        for step in range(3):
            part = part + r["r2_dst"][u][step].astype(F32)
        for i in range(8):
            r["r3_src"][u][i] = part[2 * i : 2 * i + 2].astype(BF16)
        for step in (2, 1, 3, 0):
            first = lax.rem(here[axes(u)[0]] + step, SIDE)
            for flip in range(2):
                if step or flip:
                    send(
                        r["r3_src"][u].at[first * 2 + lax.rem(core + flip, 2)],
                        r["r3_dst"][u].at[core * SIDE + here[axes(u)[0]]],
                        r["r3_send"].at[u],
                        r["r3_recv"].at[u],
                        device(axes(u)[0], step, flip),
                    )
        r["r3_dst"][u][pl.ds(core * SIDE + here[axes(u)[0]], 1)] = r["r3_src"][u][pl.ds(line_slot(u), 1)]
    for u in range(n):
        wait_all(r["sib_out"][u], r["r0_send"].at[u])
        wait_all(r["r1_dst"][u], r["r1_send"].at[u])
        wait_all(r["r2_dst"][u], r["r2_send"].at[u])
        wait_all(r["r3_dst"][u].at[pl.ds(0, 7)], r["r3_send"].at[u])
    for u in range(n):
        wait_all(r["r3_dst"][u].at[pl.ds(0, 7)], r["r3_recv"].at[u])
        for h in range(2):
            part = r["r3_dst"][u][h * SIDE].astype(F32)
            for i in range(1, SIDE):
                part = part + r["r3_dst"][u][h * SIDE + i].astype(F32)
            out[:, pl.ds(offsets[u] + h * width[u], width[u])] = part.astype(BF16)


def layer(tokens, gates, node_set, w_gate, w_up, w_down):
    _, width = widths()
    n = len(UNITS)
    whole = [w + (LANES if u == 0 else 0) for u, w in enumerate(width)]
    dma = pltpu.SemaphoreType.DMA
    vmem = pltpu.VMEM
    depth, hidden = w_gate.shape
    scratch = dict(
        gates_v=vmem(gates.shape, BF16),
        set_v=vmem(node_set.shape, jnp.int32),
        wg_v=vmem(w_gate.shape, BF16),
        wu_v=vmem(w_up.shape, BF16),
        wd_v=vmem(w_down.shape, BF16),
        src=[vmem((2, TOK, w), BF16) for w in whole],
        line=[vmem((8, TOK, w), BF16) for w in whole],
        rows=[vmem((2, ROWS, w), BF16) for w in whole],
        acc=vmem((3, ROWS, 2 * hidden), F32),
        hid=vmem((3, ROWS, hidden), BF16),
        gcol=vmem((3, ROWS, LANES), F32),
        perm=vmem((2, ROWS, ROWS), BF16),
        back=vmem((3, ROWS, ROWS), BF16),
        sib_out=[vmem((ROWS, w), BF16) for w in width],
        sib_in=[vmem((ROWS, w), BF16) for w in width],
        r1_src=[vmem((ROWS, w), BF16) for w in width],
        own=[vmem((ROWS, w), F32) for w in width],
        r1_dst=[vmem((SIDE, 3, LINE_ROWS, w), BF16) for w in width],
        r2_src=[vmem((3, LINE_ROWS, w), BF16) for w in width],
        r2_own=[vmem((LINE_ROWS, w), F32) for w in width],
        r2_dst=[vmem((3, LINE_ROWS, w), BF16) for w in width],
        r3_src=[vmem((8, TOK, w), BF16) for w in width],
        r3_dst=[vmem((8, TOK, w), BF16) for w in width],
        load_sem=dma((3,)),
        tok_sem=dma((n, 2)),
        small_sem=dma((2,)),
        p1_send=dma((n,)),
        p1_recv=dma((n,)),
        p2_send=dma((n,)),
        p2_recv=dma((n, 3)),
        p3_send=dma((n,)),
        p3_recv=dma((n, 3)),
        s_send=dma((n,)),
        s_recv=dma((n, 4)),
        r0_send=dma((n,)),
        r0_recv=dma((n, SIDE)),
        r1_send=dma((n,)),
        r1_recv=dma((n, SIDE)),
        r2_send=dma((n,)),
        r2_recv=dma((n,)),
        r3_send=dma((n,)),
        r3_recv=dma((n,)),
    )
    return pl.pallas_call(
        kernel,
        out_shape=jax.ShapeDtypeStruct(tokens.shape, BF16),
        in_specs=[pl.BlockSpec(memory_space=pl.ANY)] * 6,
        out_specs=pl.BlockSpec(memory_space=pltpu.VMEM),
        scratch_shapes=scratch,
        compiler_params=pltpu.CompilerParams(
            collective_id=0, has_side_effects=True, vmem_limit_bytes=64 << 20
        ),
    )(tokens, gates, node_set, w_gate, w_up, w_down)


def solution(mesh):
    rows, columns = P(("node", "local"), None), P(None, ("node", "local"))
    return jax.shard_map(
        layer,
        mesh=mesh,
        in_specs=(rows, rows, rows, columns, columns, rows),
        out_specs=rows,
        check_vma=False,
    )
```

time: 208 us -> 48.7 us (0.23)
  blocking collectives: 90.7 us -> 0 us
  waiting for transfers between devices: 55.2 us -> 0 us
  Pallas kernels: 0 us -> 47.2 us
  local copies, waits for them, and re-layouts: 23.8 us -> 1.38 us
  matrix products: 17.7 us -> 0 us
  starting transfers between devices: 16.9 us -> 0 us
  other arithmetic: 2.49 us -> 0 us
    all_to_all x1 -> x0, blocking collectives: 90.7 us -> none  [body(): lax.all_to_all(partial_value.reshape(flat_shape), ('node', 'local'), spli...]
    all_to_all x2 -> x0, waiting for transfers between devices: 55.2 us -> none  [the longest x1 46.4 us: body(): lax.all_to_all(wide_in, ('node', 'local'), split_axis=0, concat_axis=0, t...]
    pallas_call x0 -> x1, Pallas kernels: none -> 47.2 us  [layer(): pl.pallas_call(kernel, out_shape=jax.ShapeDtypeStruct(tokens.shape, BF16)...]
    reshape x3 -> x0, local copies, waits for them, and re-layouts: 18.4 us -> none  [the longest x1 9.26 us: body(): partial_value.reshape(flat_shape)]
    dot_general x6 -> x0, matrix products: 17.7 us -> none  [the longest x1 11.2 us: expert_output(): jnp.dot(hidden_act, part_down, preferred_element_type=jnp.float32)]
    all_to_all x2 -> x0, starting transfers between devices: 16.9 us -> none  [the longest x1 11.5 us: body(): lax.all_to_all(wide_gate, ('node', 'local'), split_axis=0, concat_axis=0,...]
    broadcast_in_dim x3 -> x0, local copies, waits for them, and re-layouts: 4.47 us -> none  [the longest x2 3.81 us: body(): wide_in = jnp.broadcast_to(send_in[:, None], wide_shape).reshape(flat_shape)]
    reduce_sum x3 -> x0, other arithmetic: 2.43 us -> none  [the longest x1 1.57 us: body(): returned = jnp.sum(arrived.reshape(wide_shape), axis=1)]
  transfers between devices with their start and end apart: 2 -> 0, of which waited for: 2 -> 0; matrix products, arithmetic and copies ran while one was open for 1% -> 0% of each run, Pallas kernels for 0% -> 0%
where the time goes in v1:
time: 48.7 us; the launch traced here: 48.6 us
  Pallas kernels  47.2 us (97%)
  local copies, waits for them, and re-layouts  1.38 us (3%)
    pallas_call x1, Pallas kernels, layer(): pl.pallas_call(kernel, out_shape=jax.ShapeDtypeStruct(tokens.shape, BF16)...  47.2 us
    unnamed x1, local copies, waits for them, and re-layouts  1.38 us

profile of v1, /device:TPU:1, one launch (start us, length us, event | category | flops | bytes accessed | tf_op | source)
XLA Modules:
  0.0 48.6 jit_solution(16046883425698238239)
XLA Ops:
  0.0 47.2 %shard_map.64 = bf16[2,7168]{1,0:T(2,128)(2,1)} custom-call(bf16[2,7168]{1,0:T(2,128)(2,1)} %tok.1, bf16[2,8]{1,0:T(2,128)(2,1)} %gates.1, s32[2,4]{1,0:T(2,128)} %node_set.1, bf16[7168,256]{1,0:T(8,128)(2,1)} %wg.1, bf16[7168,256]{1,0:T(8,128)(2,1)} %wu.1, bf16[256,7168]{1,0:T(8,128)(2,1)} %wd.1), custom_call_target="tpu_custom_call" | custom-call | tf_op jit(solution)/shard_map/pallas_call | solution.py:352
  47.2 1.4 %copy.8 = bf16[2,7168]{1,0:T(2,128)(2,1)} copy(bf16[2,7168]{1,0:T(2,128)(2,1)} %shard_map.64) | data formatting | bytes 57344

commit v2 on v1

--- a/solution.py
+++ b/solution.py
@@ -16,7 +16,8 @@
 LANES = 128
 AHEAD = (2, 1, 3, 0)
 ORDERS = ("xyz", "yzx", "zxy")
-UNITS = ((0, 10), (1, 9), (2, 9))
+UNITS = ((0, 9), (1, 10), (2, 9))
+GATED = 0
 F32, BF16 = jnp.float32, jnp.bfloat16
 
 
@@ -28,12 +29,10 @@
     return offsets, [blocks * LANES for _, blocks in UNITS]
 
 
-def row_of(order, at, by_plane):
-    low = at & 3
-    place = dict(x=(at >> 2) & 3, y=(at >> 4) & 3, z=(at >> 6) & 3)
+def row_of(order, at):
+    place = dict(x=(at >> 2) & 3, z=(at >> 4) & 3, y=(at >> 6) & 3)
     first, second, third = (place[axis] for axis in ORDERS[order])
-    slow, fast = (third, second) if by_plane else (second, third)
-    return (((slow * SIDE + fast) * SIDE + first) << 2) + low
+    return (((second * SIDE + third) * SIDE + first) << 2) + (at & 3)
 
 
 def kernel(tok, gates, node_set, wg, wu, wd, out, **r):
@@ -77,9 +76,6 @@
     partners.append(("x", 0, 1))
     for partner in partners:
         pl.semaphore_signal(barrier, inc=1, device_id=device(*partner), device_id_type=MESH)
-    for copy in loads:
-        copy.start()
-
     for copy in small:
         copy.wait()
     lane = lax.broadcasted_iota(jnp.int32, (TOK, LANES), 1)
@@ -89,7 +85,7 @@
         pair = jnp.where(lane % 2 == 0, gate_v[:, 2 * j : 2 * j + 1], gate_v[:, 2 * j + 1 : 2 * j + 2])
         table = table + jnp.where(set_v[:, j : j + 1] == lane // 2, pair, 0.0)
     for h in range(2):
-        r["src"][0][h, :, width[0] :] = table.astype(BF16)
+        r["src"][GATED][h, :, width[GATED] :] = table.astype(BF16)
     for copy in own:
         copy.wait()
     pl.semaphore_wait(barrier, len(partners))
@@ -123,50 +119,49 @@
     def wait_all(ref, sem):
         pltpu.make_async_copy(ref, ref, sem).wait()
 
+    for copy in loads:
+        copy.start()
     down_at = lax.broadcasted_iota(jnp.int32, (ROWS, ROWS), 0)
     across = lax.broadcasted_iota(jnp.int32, (ROWS, ROWS), 1)
     for o in (1, 2):
-        r["perm"][o - 1] = (row_of(o, down_at, True) == across).astype(F32).astype(BF16)
-    for o in range(3):
-        r["back"][o] = (row_of(o, across, False) == down_at).astype(F32).astype(BF16)
-    def plane_row(u):
-        return here[axes(u)[2]] * PLANE_ROWS
-
-    def line_block(u, back):
-        second = lax.rem(here[axes(u)[1]] + SIDE - back, SIDE)
-        return r["rows"][u].at[0, pl.ds(pl.multiple_of(plane_row(u) + second * LINE_ROWS, LINE_ROWS), LINE_ROWS)]
-
-    def plane_block(u, half, back):
-        third = lax.rem(here[axes(u)[2]] + SIDE - back, SIDE)
-        return r["rows"][u].at[half, pl.ds(pl.multiple_of(third * PLANE_ROWS, PLANE_ROWS), PLANE_ROWS)]
+        r["perm"][o - 1] = (row_of(o, down_at) == across).astype(F32).astype(BF16)
+        r["back"][o - 1] = (row_of(o, across) == down_at).astype(F32).astype(BF16)
+    def second_block(u, ahead):
+        second = lax.rem(here[axes(u)[1]] + ahead, SIDE)
+        return pl.ds(pl.multiple_of(second * PLANE_ROWS, PLANE_ROWS), PLANE_ROWS)
+
+    def third_block(u, ahead, step):
+        second = lax.rem(here[axes(u)[1]] + ahead, SIDE)
+        third = lax.rem(here[axes(u)[2]] + step, SIDE)
+        return pl.ds(pl.multiple_of(second * PLANE_ROWS + third * LINE_ROWS, LINE_ROWS), LINE_ROWS)
 
     def gather3(u, back):
+        view = r["rows"][u].at[0, third_block(u, SIDE - back, 0)]
         for step in (2, 1, 3):
-            view = line_block(u, back)
-            send(view, view, r["p3_send"].at[u], r["p3_recv"].at[u, step - 1], device(axes(u)[2], step, 0))
+            send(view, view, r["p3_send"].at[u], r["p3_recv"].at[u, back], device(axes(u)[2], step, 0))
 
     for u in range(n):
         wait_all(r["line"][u].at[pl.ds(0, 7)], r["p1_recv"].at[u])
         block = jnp.concatenate([r["line"][u][i].astype(F32) for i in range(8)], axis=0)
-        view = line_block(u, 0)
+        view = r["rows"][u].at[0, third_block(u, 0, 0)]
         view[...] = block.astype(BF16)
         for step in (2, 1, 3):
             send(view, view, r["p2_send"].at[u], r["p2_recv"].at[u, step - 1], device(axes(u)[1], step, 0))
     for u in range(n):
         gather3(u, 0)
-    for step in (1, 3, 2):
-        for u in range(n):
-            wait_all(line_block(u, step), r["p2_recv"].at[u, step - 1])
-            gather3(u, step)
-    for step in (0, 1, 3, 2):
-        for u in range(n):
-            if step:
-                wait_all(plane_block(u, 0, step), r["p3_recv"].at[u, step - 1])
+    for back in (1, 3, 2):
+        for u in range(n):
+            wait_all(r["rows"][u].at[0, pl.ds(0, LINE_ROWS)], r["p2_recv"].at[u, back - 1])
+            gather3(u, back)
+    for back in (0, 1, 3, 2):
+        for u in range(n):
+            wait_all(r["rows"][u].at[0, pl.ds(0, 3 * LINE_ROWS)], r["p3_recv"].at[u, back])
+            at = second_block(u, SIDE - back)
             send(
-                plane_block(u, 0, step),
-                plane_block(u, 1, step),
+                r["rows"][u].at[0, at],
+                r["rows"][u].at[1, at],
                 r["s_send"].at[u],
-                r["s_recv"].at[u, step],
+                r["s_recv"].at[u, back],
                 device("x", 0, 1),
             )
     for copy in loads[:2]:
@@ -188,10 +183,10 @@
 
     expert = node * 2 + local // 8
     lane = lax.broadcasted_iota(jnp.int32, (ROWS, LANES), 1)
-    table = r["rows"][0][0, :, width[0] :]
+    table = r["rows"][GATED][0, :, width[GATED] :]
     for o in range(3):
-        here_table = jnp.dot(r["back"][o], table, preferred_element_type=F32)
-        column = jnp.sum(jnp.where(lane == expert, here_table, 0.0), axis=1, keepdims=True)
+        here_table = table if o == 0 else jnp.dot(r["back"][o - 1], table, preferred_element_type=F32)
+        column = jnp.sum(jnp.where(lane == expert, here_table.astype(F32), 0.0), axis=1, keepdims=True)
         r["gcol"][o] = jnp.broadcast_to(column, (ROWS, LANES))
 
     total = r["acc"][0]
@@ -202,46 +197,47 @@
         total = total + jnp.dot(r["perm"][o - 1], low, preferred_element_type=F32)
     gate_pre, up_pre = total[:, :256], total[:, 256:]
     hidden = (gate_pre * jax.nn.sigmoid(gate_pre) * up_pre).astype(BF16)
-    for o in range(3):
-        r["hid"][o] = jnp.dot(r["back"][o], hidden, preferred_element_type=F32).astype(BF16)
+    r["hid"][0] = hidden
+    for o in (1, 2):
+        r["hid"][o] = jnp.dot(r["back"][o - 1], hidden, preferred_element_type=F32).astype(BF16)
     loads[2].wait()
 
     def down(u, half):
         o = UNITS[u][0]
         columns = pl.ds(pl.multiple_of(offsets[u] + half * width[u], LANES), width[u])
         part = jnp.dot(r["hid"][o], r["wd_v"][:, columns], preferred_element_type=F32)
-        return part * r["gcol"][o][:, :1]
-
-    def second_block(u, ahead):
-        second = lax.rem(here[axes(u)[1]] + ahead, SIDE)
-        return pl.ds(pl.multiple_of(second * PLANE_ROWS, PLANE_ROWS), PLANE_ROWS)
-
-    def third_block(u, ahead, step):
-        second = lax.rem(here[axes(u)[1]] + ahead, SIDE)
-        third = lax.rem(here[axes(u)[2]] + step, SIDE)
-        return pl.ds(pl.multiple_of(second * PLANE_ROWS + third * LINE_ROWS, LINE_ROWS), LINE_ROWS)
+        return part * jnp.concatenate([r["gcol"][o]] * UNITS[u][1], axis=1)
+
+    def reduce0(u, ahead):
+        at = second_block(u, ahead)
+        send(r["sib_out"][u].at[at], r["sib_in"][u].at[at], r["r0_send"].at[u], r["r0_recv"].at[u, ahead], device("x", 0, 1))
 
     for u in range(n):
         r["sib_out"][u][...] = down(u, 1 - core).astype(BF16)
-    for ahead in AHEAD:
-        for u in range(n):
-            at = second_block(u, ahead)
-            send(r["sib_out"][u].at[at], r["sib_in"][u].at[at], r["r0_send"].at[u], r["r0_recv"].at[u, ahead], device("x", 0, 1))
+        reduce0(u, AHEAD[0])
+    for ahead in AHEAD[1:]:
+        for u in range(n):
+            reduce0(u, ahead)
+
+    def reduce1(u, ahead):
+        at = second_block(u, ahead)
+        wait_all(r["sib_in"][u].at[at], r["r0_recv"].at[u, ahead])
+        r["r1_src"][u][at, :] = (r["own"][u][at, :] + r["sib_in"][u][at, :].astype(F32)).astype(BF16)
+        for step in (2, 1, 3):
+            send(
+                r["r1_src"][u].at[third_block(u, ahead, step)],
+                r["r1_dst"][u].at[ahead, step - 1],
+                r["r1_send"].at[u],
+                r["r1_recv"].at[u, ahead],
+                device(axes(u)[2], step, 0),
+            )
+
     for u in range(n):
         r["own"][u][...] = down(u, core)
-    for ahead in AHEAD:
-        for u in range(n):
-            at = second_block(u, ahead)
-            wait_all(r["sib_in"][u].at[at], r["r0_recv"].at[u, ahead])
-            r["r1_src"][u][at, :] = (r["own"][u][at, :] + r["sib_in"][u][at, :].astype(F32)).astype(BF16)
-            for step in (2, 1, 3):
-                send(
-                    r["r1_src"][u].at[third_block(u, ahead, step)],
-                    r["r1_dst"][u].at[ahead, step - 1],
-                    r["r1_send"].at[u],
-                    r["r1_recv"].at[u, ahead],
-                    device(axes(u)[2], step, 0),
-                )
+        reduce1(u, AHEAD[0])
+    for ahead in AHEAD[1:]:
+        for u in range(n):
+            reduce1(u, ahead)
     for u in range(n):
         wait_all(r["line"][u].at[pl.ds(0, 7)], r["p1_send"].at[u])
         wait_all(r["rows"][u].at[0, pl.ds(0, 3 * LINE_ROWS)], r["p2_send"].at[u])
@@ -301,7 +297,7 @@
 def layer(tokens, gates, node_set, w_gate, w_up, w_down):
     _, width = widths()
     n = len(UNITS)
-    whole = [w + (LANES if u == 0 else 0) for u, w in enumerate(width)]
+    whole = [w + (LANES if u == GATED else 0) for u, w in enumerate(width)]
     dma = pltpu.SemaphoreType.DMA
     vmem = pltpu.VMEM
     depth, hidden = w_gate.shape
@@ -318,7 +314,7 @@
         hid=vmem((3, ROWS, hidden), BF16),
         gcol=vmem((3, ROWS, LANES), F32),
         perm=vmem((2, ROWS, ROWS), BF16),
-        back=vmem((3, ROWS, ROWS), BF16),
+        back=vmem((2, ROWS, ROWS), BF16),
         sib_out=[vmem((ROWS, w), BF16) for w in width],
         sib_in=[vmem((ROWS, w), BF16) for w in width],
         r1_src=[vmem((ROWS, w), BF16) for w in width],
@@ -337,9 +333,9 @@
         p2_send=dma((n,)),
         p2_recv=dma((n, 3)),
         p3_send=dma((n,)),
-        p3_recv=dma((n, 3)),
+        p3_recv=dma((n, SIDE)),
         s_send=dma((n,)),
-        s_recv=dma((n, 4)),
+        s_recv=dma((n, SIDE)),
         r0_send=dma((n,)),
         r0_recv=dma((n, SIDE)),
         r1_send=dma((n,)),
@@ -356,9 +352,9 @@
         out_specs=pl.BlockSpec(memory_space=pltpu.VMEM),
         scratch_shapes=scratch,
         compiler_params=pltpu.CompilerParams(
-            collective_id=0, has_side_effects=True, vmem_limit_bytes=64 << 20
+            collective_id=0, has_side_effects=True, vmem_limit_bytes=48 << 20
         ),
-    )(tokens, gates, node_set, w_gate, w_up, w_down)
+    )(*[pltpu.with_memory_space_constraint(a, pltpu.HBM) for a in (tokens, gates, node_set, w_gate, w_up, w_down)])
 
 
 def solution(mesh):

time: 48.7 us -> 45.9 us (0.943)
  Pallas kernels: 47.2 us -> 45.1 us
  local copies, waits for them, and re-layouts: 1.38 us -> 0.61 us
    pallas_call x1, Pallas kernels: 47.2 us -> 45.1 us  [layer(): pl.pallas_call(kernel, out_shape=jax.ShapeDtypeStruct(tokens.shape, BF16)...]
    unnamed x1, local copies, waits for them, and re-layouts: 1.38 us -> 0.61 us
where the time goes in v2:
time: 45.9 us; the launch traced here: 45.8 us
  Pallas kernels  45.1 us (98%)
  local copies, waits for them, and re-layouts  0.61 us (1%)
    pallas_call x1, Pallas kernels, layer(): pl.pallas_call(kernel, out_shape=jax.ShapeDtypeStruct(tokens.shape, BF16)...  45.1 us

profile of v2, /device:TPU:1, one launch (start us, length us, event | category | flops | bytes accessed | tf_op | source)
XLA Modules:
  0.0 45.8 jit_solution(13942585001758022028)
XLA Ops:
  0.0 45.1 %shard_map.64 = bf16[2,7168]{1,0:T(2,128)(2,1)S(1)} custom-call(bf16[2,7168]{1,0:T(2,128)(2,1)} %tok.1, bf16[2,8]{1,0:T(2,128)(2,1)} %gates.1, s32[2,4]{1,0:T(2,128)} %node_set.1, bf16[7168,256]{1,0:T(8,128)(2,1)} %wg.1, bf16[7168,256]{1,0:T(8,128)(2,1)} %wu.1, bf16[256,7168]{1,0:T(8,128)(2,1)} %wd.1), custom_call_target="tpu_custom_call" | custom-call | tf_op jit(solution)/shard_map/pallas_call | solution.py:348
  45.2 0.6 %copy.8 = bf16[2,7168]{1,0:T(2,128)(2,1)} copy(bf16[2,7168]{1,0:T(2,128)(2,1)S(1)} %shard_map.64) | data formatting | bytes 57344

commit v3 on v2

--- a/solution.py
+++ b/solution.py
@@ -14,7 +14,11 @@
 LINE_ROWS = 16
 PLANE_ROWS = 64
 LANES = 128
-AHEAD = (2, 1, 3, 0)
+TURNS = dict(
+    x=((0, 2, 1, 3), (0, 3, 2, 1), (0, 3, 1, 2), (0, 1, 2, 3)),
+    y=((1, 2, 3, 0), (1, 3, 0, 2), (1, 0, 3, 2), (1, 0, 2, 3)),
+    z=((2, 1, 3, 0), (3, 2, 0, 1), (0, 3, 1, 2), (1, 0, 2, 3)),
+)
 ORDERS = ("xyz", "yzx", "zxy")
 UNITS = ((0, 9), (1, 10), (2, 9))
 GATED = 0
@@ -49,11 +53,15 @@
         other = lax.rem(core + flip, 2)
         return (at["z"] * 2 + other, at["x"] * SIDE + at["y"])
 
+    depth_at = [sum(width[:u]) for u in range(n)]
     loads = [
         pltpu.make_async_copy(wg, r["wg_v"], r["load_sem"].at[0]),
         pltpu.make_async_copy(wu, r["wu_v"], r["load_sem"].at[1]),
-        pltpu.make_async_copy(wd, r["wd_v"], r["load_sem"].at[2]),
     ]
+    for u in range(n):
+        mine = pl.ds(pl.multiple_of(offsets[u] + core * width[u], LANES), width[u])
+        there = pl.ds(depth_at[u], width[u])
+        loads.append(pltpu.make_async_copy(wd.at[:, mine], r["w2"].at[0, :, there], r["load_sem"].at[2]))
     small = [
         pltpu.make_async_copy(gates, r["gates_v"], r["small_sem"].at[0]),
         pltpu.make_async_copy(node_set, r["set_v"], r["small_sem"].at[1]),
@@ -121,6 +129,10 @@
 
     for copy in loads:
         copy.start()
+    for u in range(n):
+        other = pl.ds(pl.multiple_of(offsets[u] + (1 - core) * width[u], LANES), width[u])
+        there = pl.ds(depth_at[u], width[u])
+        send(wd.at[:, other], r["w2"].at[1, :, there], r["w_send"], r["w_recv"], device("x", 0, 1))
     down_at = lax.broadcasted_iota(jnp.int32, (ROWS, ROWS), 0)
     across = lax.broadcasted_iota(jnp.int32, (ROWS, ROWS), 1)
     for o in (1, 2):
@@ -181,13 +193,14 @@
                 first = which == 0 and all(UNITS[v][0] != o for v in range(u))
                 r["acc"][o, :, columns] = part if first else r["acc"][o, :, columns] + part
 
-    expert = node * 2 + local // 8
     lane = lax.broadcasted_iota(jnp.int32, (ROWS, LANES), 1)
     table = r["rows"][GATED][0, :, width[GATED] :]
     for o in range(3):
         here_table = table if o == 0 else jnp.dot(r["back"][o - 1], table, preferred_element_type=F32)
-        column = jnp.sum(jnp.where(lane == expert, here_table.astype(F32), 0.0), axis=1, keepdims=True)
-        r["gcol"][o] = jnp.broadcast_to(column, (ROWS, LANES))
+        for who in range(2):
+            expert = (here["z"] * 2 + lax.rem(core + who, 2)) * 2 + local // 8
+            column = jnp.sum(jnp.where(lane == expert, here_table.astype(F32), 0.0), axis=1, keepdims=True)
+            r["gcol"][who, o] = jnp.broadcast_to(column, (ROWS, LANES))
 
     total = r["acc"][0]
     for o in (1, 2):
@@ -197,71 +210,84 @@
         total = total + jnp.dot(r["perm"][o - 1], low, preferred_element_type=F32)
     gate_pre, up_pre = total[:, :256], total[:, 256:]
     hidden = (gate_pre * jax.nn.sigmoid(gate_pre) * up_pre).astype(BF16)
-    r["hid"][0] = hidden
-    for o in (1, 2):
-        r["hid"][o] = jnp.dot(r["back"][o - 1], hidden, preferred_element_type=F32).astype(BF16)
-    loads[2].wait()
-
-    def down(u, half):
+    r["hid"][0, 0] = hidden
+    send(r["hid"].at[0, 0], r["hid"].at[1, 0], r["h_send"], r["h_recv"], device("x", 0, 1))
+
+    def down(u, who):
         o = UNITS[u][0]
-        columns = pl.ds(pl.multiple_of(offsets[u] + half * width[u], LANES), width[u])
-        part = jnp.dot(r["hid"][o], r["wd_v"][:, columns], preferred_element_type=F32)
-        return part * jnp.concatenate([r["gcol"][o]] * UNITS[u][1], axis=1)
-
-    def reduce0(u, ahead):
-        at = second_block(u, ahead)
-        send(r["sib_out"][u].at[at], r["sib_in"][u].at[at], r["r0_send"].at[u], r["r0_recv"].at[u, ahead], device("x", 0, 1))
-
-    for u in range(n):
-        r["sib_out"][u][...] = down(u, 1 - core).astype(BF16)
-        reduce0(u, AHEAD[0])
-    for ahead in AHEAD[1:]:
-        for u in range(n):
-            reduce0(u, ahead)
-
-    def reduce1(u, ahead):
-        at = second_block(u, ahead)
-        wait_all(r["sib_in"][u].at[at], r["r0_recv"].at[u, ahead])
-        r["r1_src"][u][at, :] = (r["own"][u][at, :] + r["sib_in"][u][at, :].astype(F32)).astype(BF16)
-        for step in (2, 1, 3):
-            send(
-                r["r1_src"][u].at[third_block(u, ahead, step)],
-                r["r1_dst"][u].at[ahead, step - 1],
-                r["r1_send"].at[u],
-                r["r1_recv"].at[u, ahead],
-                device(axes(u)[2], step, 0),
-            )
-
-    for u in range(n):
-        r["own"][u][...] = down(u, core)
-        reduce1(u, AHEAD[0])
-    for ahead in AHEAD[1:]:
-        for u in range(n):
-            reduce1(u, ahead)
+        weight = r["w2"][who, :, depth_at[u] : depth_at[u] + width[u]]
+        part = jnp.dot(r["hid"][who, o], weight, preferred_element_type=F32)
+        return part * jnp.concatenate([r["gcol"][who, o]] * UNITS[u][1], axis=1)
+
+    def reorder(who):
+        for o in (1, 2):
+            r["hid"][who, o] = jnp.dot(r["back"][o - 1], r["hid"][who, 0], preferred_element_type=F32).astype(BF16)
+
+    reorder(0)
+    wait_all(r["w2"].at[0], r["load_sem"].at[2])
+    wait_all(r["w2"].at[1], r["w_recv"])
+    for u in range(n):
+        r["own"][u][...] = down(u, 0)
+    wait_all(r["hid"].at[1, 0], r["h_recv"])
+    reorder(1)
+    def turn(u, slot):
+        axis = axes(u)[1]
+        place = TURNS[axis][0][slot]
+        for i in range(1, SIDE):
+            place = jnp.where(here[axis] == i, TURNS[axis][i][slot], place)
+        return place
+
+    def third_rows(u, place, step):
+        third = lax.rem(here[axes(u)[2]] + step, SIDE)
+        return pl.ds(pl.multiple_of(place * PLANE_ROWS + third * LINE_ROWS, LINE_ROWS), LINE_ROWS)
+
+    for u in range(n):
+        total = r["own"][u][...] + down(u, 1)
+        r["own"][u][...] = total
+        r["r1_src"][u][...] = total.astype(BF16)
+        for slot in range(SIDE):
+            for step in (2, 1, 3):
+                send(
+                    r["r1_src"][u].at[third_rows(u, turn(u, slot), step)],
+                    r["r1_dst"][u].at[slot, step - 1],
+                    r["r1_send"].at[u],
+                    r["r1_recv"].at[u, slot],
+                    device(axes(u)[2], step, 0),
+                )
     for u in range(n):
         wait_all(r["line"][u].at[pl.ds(0, 7)], r["p1_send"].at[u])
         wait_all(r["rows"][u].at[0, pl.ds(0, 3 * LINE_ROWS)], r["p2_send"].at[u])
         wait_all(r["rows"][u].at[0, pl.ds(0, 3 * PLANE_ROWS)], r["p3_send"].at[u])
         wait_all(r["rows"][u].at[0], r["s_send"].at[u])
-    for ahead in AHEAD:
+    wait_all(r["w2"].at[1], r["w_send"])
+    wait_all(r["hid"].at[0, 0], r["h_send"])
+    def reduce2(u, slot):
+        place = turn(u, slot)
+        wait_all(r["r1_dst"][u].at[slot], r["r1_recv"].at[u, slot])
+        part = r["own"][u][third_rows(u, place, 0), :]
+        for step in range(3):
+            part = part + r["r1_dst"][u][slot, step].astype(F32)
+        ahead = lax.rem(place + SIDE - here[axes(u)[1]], SIDE)
+
+        @pl.when(ahead == 0)
+        def _():
+            r["r2_own"][u][...] = part
+
+        @pl.when(ahead != 0)
+        def _():
+            r["r2_src"][u][slot] = part.astype(BF16)
+            send(
+                r["r2_src"][u].at[slot],
+                r["r2_dst"][u].at[ahead - 1],
+                r["r2_send"].at[u],
+                r["r2_recv"].at[u],
+                device(axes(u)[1], ahead, 0),
+            )
+
+    for slot in range(SIDE):
         for u in range(n):
-            at = third_block(u, ahead, 0)
-            wait_all(r["r1_dst"][u].at[ahead], r["r1_recv"].at[u, ahead])
-            part = r["own"][u][at, :] + r["sib_in"][u][at, :].astype(F32)
-            for step in range(3):
-                part = part + r["r1_dst"][u][ahead, step].astype(F32)
-            if ahead:
-                r["r2_src"][u][ahead - 1] = part.astype(BF16)
-                send(
-                    r["r2_src"][u].at[ahead - 1],
-                    r["r2_dst"][u].at[ahead - 1],
-                    r["r2_send"].at[u],
-                    r["r2_recv"].at[u],
-                    device(axes(u)[1], ahead, 0),
-                )
-            else:
-                r["r2_own"][u][...] = part
-    for u in range(n):
+            reduce2(u, slot)
+    def reduce3(u):
         wait_all(r["r2_dst"][u], r["r2_recv"].at[u])
         part = r["r2_own"][u][...]
         for step in range(3):
@@ -280,8 +306,12 @@
                         device(axes(u)[0], step, flip),
                     )
         r["r3_dst"][u][pl.ds(core * SIDE + here[axes(u)[0]], 1)] = r["r3_src"][u][pl.ds(line_slot(u), 1)]
-    for u in range(n):
-        wait_all(r["sib_out"][u], r["r0_send"].at[u])
+
+    for u in range(n):
+        pl.when(here[axes(u)[1]] == TURNS[axes(u)[1]][0][0])(functools.partial(reduce3, u))
+    for u in range(n):
+        pl.when(here[axes(u)[1]] != TURNS[axes(u)[1]][0][0])(functools.partial(reduce3, u))
+    for u in range(n):
         wait_all(r["r1_dst"][u], r["r1_send"].at[u])
         wait_all(r["r2_dst"][u], r["r2_send"].at[u])
         wait_all(r["r3_dst"][u].at[pl.ds(0, 7)], r["r3_send"].at[u])
@@ -306,21 +336,19 @@
         set_v=vmem(node_set.shape, jnp.int32),
         wg_v=vmem(w_gate.shape, BF16),
         wu_v=vmem(w_up.shape, BF16),
-        wd_v=vmem(w_down.shape, BF16),
+        w2=vmem((2, hidden, depth // 2), BF16),
         src=[vmem((2, TOK, w), BF16) for w in whole],
         line=[vmem((8, TOK, w), BF16) for w in whole],
         rows=[vmem((2, ROWS, w), BF16) for w in whole],
         acc=vmem((3, ROWS, 2 * hidden), F32),
-        hid=vmem((3, ROWS, hidden), BF16),
-        gcol=vmem((3, ROWS, LANES), F32),
+        hid=vmem((2, 3, ROWS, hidden), BF16),
+        gcol=vmem((2, 3, ROWS, LANES), F32),
         perm=vmem((2, ROWS, ROWS), BF16),
         back=vmem((2, ROWS, ROWS), BF16),
-        sib_out=[vmem((ROWS, w), BF16) for w in width],
-        sib_in=[vmem((ROWS, w), BF16) for w in width],
         r1_src=[vmem((ROWS, w), BF16) for w in width],
         own=[vmem((ROWS, w), F32) for w in width],
         r1_dst=[vmem((SIDE, 3, LINE_ROWS, w), BF16) for w in width],
-        r2_src=[vmem((3, LINE_ROWS, w), BF16) for w in width],
+        r2_src=[vmem((SIDE, LINE_ROWS, w), BF16) for w in width],
         r2_own=[vmem((LINE_ROWS, w), F32) for w in width],
         r2_dst=[vmem((3, LINE_ROWS, w), BF16) for w in width],
         r3_src=[vmem((8, TOK, w), BF16) for w in width],
@@ -336,8 +364,10 @@
         p3_recv=dma((n, SIDE)),
         s_send=dma((n,)),
         s_recv=dma((n, SIDE)),
-        r0_send=dma((n,)),
-        r0_recv=dma((n, SIDE)),
+        w_send=dma,
+        w_recv=dma,
+        h_send=dma,
+        h_recv=dma,
         r1_send=dma((n,)),
         r1_recv=dma((n, SIDE)),
         r2_send=dma((n,)),

time: 45.9 us -> 45 us (0.980)
  Pallas kernels: 45.1 us -> 44.2 us
    pallas_call x1, Pallas kernels: 45.1 us -> 44.2 us  [layer(): pl.pallas_call(kernel, out_shape=jax.ShapeDtypeStruct(tokens.shape, BF16)...]
where the time goes in v3:
time: 45 us; the launch traced here: 44.8 us
  Pallas kernels  44.2 us (98%)
  local copies, waits for them, and re-layouts  0.61 us (1%)
    pallas_call x1, Pallas kernels, layer(): pl.pallas_call(kernel, out_shape=jax.ShapeDtypeStruct(tokens.shape, BF16)...  44.2 us

profile of v3, /device:TPU:1, one launch (start us, length us, event | category | flops | bytes accessed | tf_op | source)
XLA Modules:
  0.0 44.8 jit_solution(7988489144300587136)
XLA Ops:
  0.0 44.2 %shard_map.64 = bf16[2,7168]{1,0:T(2,128)(2,1)S(1)} custom-call(bf16[2,7168]{1,0:T(2,128)(2,1)} %tok.1, bf16[2,8]{1,0:T(2,128)(2,1)} %gates.1, s32[2,4]{1,0:T(2,128)} %node_set.1, bf16[7168,256]{1,0:T(8,128)(2,1)} %wg.1, bf16[7168,256]{1,0:T(8,128)(2,1)} %wu.1, bf16[256,7168]{1,0:T(8,128)(2,1)} %wd.1), custom_call_target="tpu_custom_call" | custom-call | tf_op jit(solution)/shard_map/pallas_call | solution.py:378
  44.2 0.6 %copy.8 = bf16[2,7168]{1,0:T(2,128)(2,1)} copy(bf16[2,7168]{1,0:T(2,128)(2,1)S(1)} %shard_map.64) | data formatting | bytes 57344

commit v4 on v3

--- a/solution.py
+++ b/solution.py
@@ -16,11 +16,12 @@
 LANES = 128
 TURNS = dict(
     x=((0, 2, 1, 3), (0, 3, 2, 1), (0, 3, 1, 2), (0, 1, 2, 3)),
-    y=((1, 2, 3, 0), (1, 3, 0, 2), (1, 0, 3, 2), (1, 0, 2, 3)),
+    y=((2, 1, 3, 0), (3, 2, 0, 1), (0, 3, 1, 2), (1, 0, 2, 3)),
     z=((2, 1, 3, 0), (3, 2, 0, 1), (0, 3, 1, 2), (1, 0, 2, 3)),
 )
+STARTS = dict(x=(0, 2, 1, 3), y=(1, 0, 2, 3), z=(0, 1, 2, 3))
 ORDERS = ("xyz", "yzx", "zxy")
-UNITS = ((0, 9), (1, 10), (2, 9))
+UNITS = ((0, 9), (2, 9), (1, 10))
 GATED = 0
 F32, BF16 = jnp.float32, jnp.bfloat16
 
@@ -161,12 +162,23 @@
             send(view, view, r["p2_send"].at[u], r["p2_recv"].at[u, step - 1], device(axes(u)[1], step, 0))
     for u in range(n):
         gather3(u, 0)
-    for back in (1, 3, 2):
+
+    def behind(u, slot):
+        axis = axes(u)[1]
+        place = None
+        for i in range(SIDE):
+            there = [p for p in STARTS[axis] if p != i][slot]
+            place = there if place is None else jnp.where(here[axis] == i, there, place)
+        return lax.rem(here[axis] - place + SIDE, SIDE)
+
+    for slot in range(3):
         for u in range(n):
+            back = behind(u, slot)
             wait_all(r["rows"][u].at[0, pl.ds(0, LINE_ROWS)], r["p2_recv"].at[u, back - 1])
             gather3(u, back)
-    for back in (0, 1, 3, 2):
+    for slot in range(SIDE):
         for u in range(n):
+            back = behind(u, slot - 1) if slot else 0
             wait_all(r["rows"][u].at[0, pl.ds(0, 3 * LINE_ROWS)], r["p3_recv"].at[u, back])
             at = second_block(u, SIDE - back)
             send(

time: 45 us -> 44.7 us (level)
  no operation moved by 1% of the time
where the time goes in v4:
time: 44.7 us; the launch traced here: 44.6 us
  Pallas kernels  44 us (98%)
  local copies, waits for them, and re-layouts  0.61 us (1%)
    pallas_call x1, Pallas kernels, layer(): pl.pallas_call(kernel, out_shape=jax.ShapeDtypeStruct(tokens.shape, BF16)...  44 us

profile of v4, /device:TPU:1, one launch (start us, length us, event | category | flops | bytes accessed | tf_op | source)
XLA Modules:
  0.0 44.6 jit_solution(1826355662936541589)
XLA Ops:
  0.0 44.0 %shard_map.64 = bf16[2,7168]{1,0:T(2,128)(2,1)S(1)} custom-call(bf16[2,7168]{1,0:T(2,128)(2,1)} %tok.1, bf16[2,8]{1,0:T(2,128)(2,1)} %gates.1, s32[2,4]{1,0:T(2,128)} %node_set.1, bf16[7168,256]{1,0:T(8,128)(2,1)} %wg.1, bf16[7168,256]{1,0:T(8,128)(2,1)} %wu.1, bf16[256,7168]{1,0:T(8,128)(2,1)} %wd.1), custom_call_target="tpu_custom_call" | custom-call | tf_op jit(solution)/shard_map/pallas_call | solution.py:390
  44.0 0.6 %copy.8 = bf16[2,7168]{1,0:T(2,128)(2,1)} copy(bf16[2,7168]{1,0:T(2,128)(2,1)S(1)} %shard_map.64) | data formatting | bytes 57344

commit v5 on v4

--- a/solution.py
+++ b/solution.py
@@ -112,8 +112,8 @@
     def line_slot(u):
         return here[axes(u)[0]] * 2 + core
 
-    for u in range(n):
-        for step in (1, 3, 2, 0):
+    for step in (2, 1, 3, 0):
+        for u in range(n):
             for flip in range(2):
                 if step or flip:
                     send(
@@ -123,6 +123,7 @@
                         r["p1_recv"].at[u],
                         device(axes(u)[0], step, flip),
                     )
+    for u in range(n):
         r["line"][u][pl.ds(line_slot(u), 1)] = r["src"][u][pl.ds(core, 1)]
 
     def wait_all(ref, sem):
@@ -254,9 +255,7 @@
         return pl.ds(pl.multiple_of(place * PLANE_ROWS + third * LINE_ROWS, LINE_ROWS), LINE_ROWS)
 
     for u in range(n):
-        total = r["own"][u][...] + down(u, 1)
-        r["own"][u][...] = total
-        r["r1_src"][u][...] = total.astype(BF16)
+        r["r1_src"][u][...] = (r["own"][u][...] + down(u, 1)).astype(BF16)
         for slot in range(SIDE):
             for step in (2, 1, 3):
                 send(
@@ -276,7 +275,7 @@
     def reduce2(u, slot):
         place = turn(u, slot)
         wait_all(r["r1_dst"][u].at[slot], r["r1_recv"].at[u, slot])
-        part = r["own"][u][third_rows(u, place, 0), :]
+        part = r["r1_src"][u][third_rows(u, place, 0), :].astype(F32)
         for step in range(3):
             part = part + r["r1_dst"][u][slot, step].astype(F32)
         ahead = lax.rem(place + SIDE - here[axes(u)[1]], SIDE)

time: 44.7 us -> 44.6 us (level)
  no operation moved by 1% of the time
where the time goes in v5:
time: 44.6 us; the launch traced here: 44.5 us
  Pallas kernels  43.8 us (98%)
  local copies, waits for them, and re-layouts  0.61 us (1%)
    pallas_call x1, Pallas kernels, layer(): pl.pallas_call(kernel, out_shape=jax.ShapeDtypeStruct(tokens.shape, BF16)...  43.8 us

profile of v5, /device:TPU:1, one launch (start us, length us, event | category | flops | bytes accessed | tf_op | source)
XLA Modules:
  0.0 44.5 jit_solution(7847071913716607570)
XLA Ops:
  0.0 43.8 %shard_map.64 = bf16[2,7168]{1,0:T(2,128)(2,1)S(1)} custom-call(bf16[2,7168]{1,0:T(2,128)(2,1)} %tok.1, bf16[2,8]{1,0:T(2,128)(2,1)} %gates.1, s32[2,4]{1,0:T(2,128)} %node_set.1, bf16[7168,256]{1,0:T(8,128)(2,1)} %wg.1, bf16[7168,256]{1,0:T(8,128)(2,1)} %wu.1, bf16[256,7168]{1,0:T(8,128)(2,1)} %wd.1), custom_call_target="tpu_custom_call" | custom-call | tf_op jit(solution)/shard_map/pallas_call | solution.py:389
  43.8 0.6 %copy.8 = bf16[2,7168]{1,0:T(2,128)(2,1)} copy(bf16[2,7168]{1,0:T(2,128)(2,1)S(1)} %shard_map.64) | data formatting | bytes 57344

commit v6 on v5

--- a/solution.py
+++ b/solution.py
@@ -81,7 +81,7 @@
         copy.start()
 
     barrier = pltpu.get_barrier_semaphore()
-    partners = [(axis, step, flip) for axis in "xyz" for step in range(1, SIDE) for flip in range(2)]
+    partners = [(axis, step, flip) for step in (2, 1, 3) for axis in "xyz" for flip in range(2)]
     partners.append(("x", 0, 1))
     for partner in partners:
         pl.semaphore_signal(barrier, inc=1, device_id=device(*partner), device_id_type=MESH)

time: 44.6 us -> 44.6 us (level)
  no operation moved by 1% of the time
where the time goes in v6:
time: 44.6 us; the launch traced here: 44.4 us
  Pallas kernels  43.8 us (98%)
  local copies, waits for them, and re-layouts  0.61 us (1%)
    pallas_call x1, Pallas kernels, layer(): pl.pallas_call(kernel, out_shape=jax.ShapeDtypeStruct(tokens.shape, BF16)...  43.8 us

profile of v6, /device:TPU:1, one launch (start us, length us, event | category | flops | bytes accessed | tf_op | source)
XLA Modules:
  0.0 44.4 jit_solution(6988986894564294057)
XLA Ops:
  0.0 43.8 %shard_map.64 = bf16[2,7168]{1,0:T(2,128)(2,1)S(1)} custom-call(bf16[2,7168]{1,0:T(2,128)(2,1)} %tok.1, bf16[2,8]{1,0:T(2,128)(2,1)} %gates.1, s32[2,4]{1,0:T(2,128)} %node_set.1, bf16[7168,256]{1,0:T(8,128)(2,1)} %wg.1, bf16[7168,256]{1,0:T(8,128)(2,1)} %wu.1, bf16[256,7168]{1,0:T(8,128)(2,1)} %wd.1), custom_call_target="tpu_custom_call" | custom-call | tf_op jit(solution)/shard_map/pallas_call | solution.py:389
  43.8 0.6 %copy.8 = bf16[2,7168]{1,0:T(2,128)(2,1)} copy(bf16[2,7168]{1,0:T(2,128)(2,1)S(1)} %shard_map.64) | data formatting | bytes 57344
